TPU v7x, 256 devices: a whole 4x4x8 slice. The times are simulated.
256 devices in a mesh: prow: 4 (over y), pcol: 64 (over z, x, core).
Axes of the slice: x: 4, y: 4, z: 8, core: 2. Of those that a mesh axis runs over, the one named last changes fastest.
Arguments:
- rhs: bfloat16 [12, 4096, 384], P(None, ('prow', 'pcol')), may hold values from -6 to 6
- factor_blocks: bfloat16 [48, 4, 64, 16, 4096], P(None, None, 'pcol', None, 'prow'), may hold values from -0.046875 to 0.046875
- diag_inverses: bfloat16 [12, 4, 64, 16, 4096], P(None, None, 'pcol', None, 'prow'), as said below
- block_index: int32 [48, 2], replicated, may hold values from 0 to 11, as said below
Outputs:
- solution: bfloat16 [12, 4096, 384], P(None, ('prow', 'pcol'))
Inputs may be any that keep to these rules, and one draw needn't show every extreme that they name: `block_index`: 48 distinct pairs (block row, block column) with column < row, listed by row and then by column. `diag_inverses`: each D_j is lower triangular (zero above the diagonal) with a positive diagonal between 0.5 and 1.
All inputs are finite; a program needn't handle non-finite values.
Results may differ from a plain program's by a relative error of at most 0.013.
Values may be sent and summed in bfloat16 or wider, within the bound.
No kernel may reach another device: no remote copies, remote signals or barrier semaphores. Data moves between devices by JAX's collectives and lax.ppermute only.
A program may use at most 64 MiB of HBM per device.

v0:
```python
import jax
import jax.numpy as jnp
from jax import lax
from jax.sharding import PartitionSpec as P


def finish_block(partial_value, rhs_piece, inverse_block):
    row_share = lax.psum_scatter(partial_value, "prow", scatter_dimension=0, tiled=True)
    residual = (rhs_piece.astype(jnp.float32) - row_share).astype(jnp.bfloat16)
    inverse_image = jnp.dot(
        inverse_block,
        lax.all_gather(residual, "pcol", axis=0, tiled=True),
        preferred_element_type=jnp.float32,
    )
    return lax.psum_scatter(inverse_image, "prow", scatter_dimension=0, tiled=True).astype(
        jnp.bfloat16
    )


def spread_block(solved):
    return lax.all_gather(solved, "pcol", axis=0, tiled=True)


def rhs_block(rhs, current, first, count):
    return lax.dynamic_slice(rhs, (current, 0, first), (1, rhs.shape[1], count))[0]


def shards(rhs, factor_blocks, diag_inverses, block_index):
    blocks, piece_rows, columns = rhs.shape
    entries = factor_blocks.shape[0]
    row_span = factor_blocks.shape[-1]
    factor = factor_blocks.reshape(entries, -1, row_span)
    inverse = diag_inverses.reshape(blocks, -1, row_span)
    owned_rows = factor.shape[1]
    block_rows = block_index[:, 0]
    block_cols = block_index[:, 1]
    numbers = jnp.arange(blocks, dtype=jnp.int32)
    groups = ((0, columns),)
    solution = jnp.zeros((blocks, piece_rows, columns), jnp.bfloat16)
    final = blocks - 1

    def inverse_at(current):
        return lax.dynamic_index_in_dim(inverse, current, 0, keepdims=False)

    row_begin = jnp.sum((block_rows[None, :] < numbers[:, None]).astype(jnp.int32), axis=1)
    row_end = jnp.sum((block_rows[None, :] <= numbers[:, None]).astype(jnp.int32), axis=1)
    gathered = jnp.zeros((blocks, row_span, columns), jnp.bfloat16)

    def row_update(current, first, count, gathered):

        def accumulate(entry, running):
            matrix = lax.dynamic_index_in_dim(factor, entry, 0, keepdims=False)
            source = lax.dynamic_slice(
                gathered, (block_cols[entry], 0, first), (1, row_span, count)
            )[0]
            return running + jnp.dot(matrix, source, preferred_element_type=jnp.float32)

        return lax.fori_loop(
            row_begin[current],
            row_end[current],
            accumulate,
            jnp.zeros((owned_rows, count), jnp.float32),
        )

    def advance(current, state):
        solution, gathered = state
        first, count = groups[0]
        partial_value = row_update(current, first, count, gathered)
        solved = finish_block(
            partial_value, rhs_block(rhs, current, first, count), inverse_at(current)
        )
        solution = lax.dynamic_update_slice(solution, solved[None], (current, 0, first))
        spread = spread_block(solved)
        gathered = lax.dynamic_update_slice(gathered, spread[None], (current, 0, first))
        return (solution, gathered)

    solution, gathered = lax.fori_loop(0, final, advance, (solution, gathered))
    first, count = groups[0]
    partial_value = row_update(final, first, count, gathered)
    solved = finish_block(partial_value, rhs[final, :, first : first + count], inverse[final])
    solution = solution.at[final, :, first : first + count].set(solved)
    return solution


def solution(mesh):
    in_specs = (
        P(None, ("prow", "pcol"), None),
        P(None, None, "pcol", None, "prow"),
        P(None, None, "pcol", None, "prow"),
        P(),
    )
    out_specs = P(None, ("prow", "pcol"), None)
    return jax.shard_map(shards, mesh=mesh, in_specs=in_specs, out_specs=out_specs, check_vma=False)
```

profile of v0, /device:TPU:1, one launch (start us, length us, event | category | flops | bytes accessed | tf_op | source)
XLA Modules:
  0.0 2173.1 jit_solution(7936921486070024520)
XLA Ops:
  14.2 1989.6 %while.49 = (s32[]{:T(128)}, bf16[12,16,384]{2,1,0:T(8,128)(2,1)S(1)}, bf16[12,1024,384]{2,1,0:T(8,128)(2,1)}, bf16[12,64,1024]{2,1,0:T(8,128)(2,1)}, bf16[12,16...) while((s32[]{:T(128)}, ...), condition=%wide.region_7.8_spmd, body=%wide.region_2.7_spmd.sunk | while | flops 100712456 | bytes 6627898 | solution.py:77
  42.9 54.0 %all_gather.20 = bf16[1024,384]{1,0:T(8,128)(2,1)S(1)} all-gather(bf16[16,384]{1,0:T(8,128)(2,1)S(1)} %fusion.29), channel_id=1, replica_groups=mesh['prow'=4,'pcol'=64] {'pcol'}, dimensions={0}, use_global_device_ids=true | all-gather | bytes 798720 | tf_op jit(solution)/shard_map/while/body/eval_jaxpr/all_gather | solution.py:12
  116.7 54.0 %all_gather.21 = bf16[1024,384]{1,0:T(8,128)(2,1)S(1)} all-gather(bf16[16,384]{1,0:T(8,128)(2,1)S(1)} %get-tuple-element.425), channel_id=1, replica_groups=mesh['prow'=4,'pcol'=64] {'pcol'}, dimensions={0}, use_global_device_ids=true | all-gather | bytes 798720 | tf_op jit(solution)/shard_map/while/body/eval_jaxpr/all_gather | solution.py:21
  192.8 54.0 %all_gather.20 = bf16[1024,384]{1,0:T(8,128)(2,1)S(1)} all-gather(bf16[16,384]{1,0:T(8,128)(2,1)S(1)} %fusion.29), channel_id=1, replica_groups=mesh['prow'=4,'pcol'=64] {'pcol'}, dimensions={0}, use_global_device_ids=true | all-gather | bytes 798720 | tf_op jit(solution)/shard_map/while/body/eval_jaxpr/all_gather | solution.py:12
  266.6 54.0 %all_gather.21 = bf16[1024,384]{1,0:T(8,128)(2,1)S(1)} all-gather(bf16[16,384]{1,0:T(8,128)(2,1)S(1)} %get-tuple-element.425), channel_id=1, replica_groups=mesh['prow'=4,'pcol'=64] {'pcol'}, dimensions={0}, use_global_device_ids=true | all-gather | bytes 798720 | tf_op jit(solution)/shard_map/while/body/eval_jaxpr/all_gather | solution.py:21
  359.4 54.0 %all_gather.20 = bf16[1024,384]{1,0:T(8,128)(2,1)S(1)} all-gather(bf16[16,384]{1,0:T(8,128)(2,1)S(1)} %fusion.29), channel_id=1, replica_groups=mesh['prow'=4,'pcol'=64] {'pcol'}, dimensions={0}, use_global_device_ids=true | all-gather | bytes 798720 | tf_op jit(solution)/shard_map/while/body/eval_jaxpr/all_gather | solution.py:12
  433.2 54.0 %all_gather.21 = bf16[1024,384]{1,0:T(8,128)(2,1)S(1)} all-gather(bf16[16,384]{1,0:T(8,128)(2,1)S(1)} %get-tuple-element.425), channel_id=1, replica_groups=mesh['prow'=4,'pcol'=64] {'pcol'}, dimensions={0}, use_global_device_ids=true | all-gather | bytes 798720 | tf_op jit(solution)/shard_map/while/body/eval_jaxpr/all_gather | solution.py:21
  525.9 54.0 %all_gather.20 = bf16[1024,384]{1,0:T(8,128)(2,1)S(1)} all-gather(bf16[16,384]{1,0:T(8,128)(2,1)S(1)} %fusion.29), channel_id=1, replica_groups=mesh['prow'=4,'pcol'=64] {'pcol'}, dimensions={0}, use_global_device_ids=true | all-gather | bytes 798720 | tf_op jit(solution)/shard_map/while/body/eval_jaxpr/all_gather | solution.py:12
  700.8 54.0 %all_gather.20 = bf16[1024,384]{1,0:T(8,128)(2,1)S(1)} all-gather(bf16[16,384]{1,0:T(8,128)(2,1)S(1)} %fusion.29), channel_id=1, replica_groups=mesh['prow'=4,'pcol'=64] {'pcol'}, dimensions={0}, use_global_device_ids=true | all-gather | bytes 798720 | tf_op jit(solution)/shard_map/while/body/eval_jaxpr/all_gather | solution.py:12
  774.6 54.0 %all_gather.21 = bf16[1024,384]{1,0:T(8,128)(2,1)S(1)} all-gather(bf16[16,384]{1,0:T(8,128)(2,1)S(1)} %get-tuple-element.425), channel_id=1, replica_groups=mesh['prow'=4,'pcol'=64] {'pcol'}, dimensions={0}, use_global_device_ids=true | all-gather | bytes 798720 | tf_op jit(solution)/shard_map/while/body/eval_jaxpr/all_gather | solution.py:21
  875.7 54.0 %all_gather.20 = bf16[1024,384]{1,0:T(8,128)(2,1)S(1)} all-gather(bf16[16,384]{1,0:T(8,128)(2,1)S(1)} %fusion.29), channel_id=1, replica_groups=mesh['prow'=4,'pcol'=64] {'pcol'}, dimensions={0}, use_global_device_ids=true | all-gather | bytes 798720 | tf_op jit(solution)/shard_map/while/body/eval_jaxpr/all_gather | solution.py:12
  949.5 54.0 %all_gather.21 = bf16[1024,384]{1,0:T(8,128)(2,1)S(1)} all-gather(bf16[16,384]{1,0:T(8,128)(2,1)S(1)} %get-tuple-element.425), channel_id=1, replica_groups=mesh['prow'=4,'pcol'=64] {'pcol'}, dimensions={0}, use_global_device_ids=true | all-gather | bytes 798720 | tf_op jit(solution)/shard_map/while/body/eval_jaxpr/all_gather | solution.py:21
  1067.3 54.0 %all_gather.20 = bf16[1024,384]{1,0:T(8,128)(2,1)S(1)} all-gather(bf16[16,384]{1,0:T(8,128)(2,1)S(1)} %fusion.29), channel_id=1, replica_groups=mesh['prow'=4,'pcol'=64] {'pcol'}, dimensions={0}, use_global_device_ids=true | all-gather | bytes 798720 | tf_op jit(solution)/shard_map/while/body/eval_jaxpr/all_gather | solution.py:12
  1141.1 54.0 %all_gather.21 = bf16[1024,384]{1,0:T(8,128)(2,1)S(1)} all-gather(bf16[16,384]{1,0:T(8,128)(2,1)S(1)} %get-tuple-element.425), channel_id=1, replica_groups=mesh['prow'=4,'pcol'=64] {'pcol'}, dimensions={0}, use_global_device_ids=true | all-gather | bytes 798720 | tf_op jit(solution)/shard_map/while/body/eval_jaxpr/all_gather | solution.py:21
  1250.5 54.0 %all_gather.20 = bf16[1024,384]{1,0:T(8,128)(2,1)S(1)} all-gather(bf16[16,384]{1,0:T(8,128)(2,1)S(1)} %fusion.29), channel_id=1, replica_groups=mesh['prow'=4,'pcol'=64] {'pcol'}, dimensions={0}, use_global_device_ids=true | all-gather | bytes 798720 | tf_op jit(solution)/shard_map/while/body/eval_jaxpr/all_gather | solution.py:12
  1324.3 54.0 %all_gather.21 = bf16[1024,384]{1,0:T(8,128)(2,1)S(1)} all-gather(bf16[16,384]{1,0:T(8,128)(2,1)S(1)} %get-tuple-element.425), channel_id=1, replica_groups=mesh['prow'=4,'pcol'=64] {'pcol'}, dimensions={0}, use_global_device_ids=true | all-gather | bytes 798720 | tf_op jit(solution)/shard_map/while/body/eval_jaxpr/all_gather | solution.py:21
  1450.3 54.0 %all_gather.20 = bf16[1024,384]{1,0:T(8,128)(2,1)S(1)} all-gather(bf16[16,384]{1,0:T(8,128)(2,1)S(1)} %fusion.29), channel_id=1, replica_groups=mesh['prow'=4,'pcol'=64] {'pcol'}, dimensions={0}, use_global_device_ids=true | all-gather | bytes 798720 | tf_op jit(solution)/shard_map/while/body/eval_jaxpr/all_gather | solution.py:12
  1650.2 54.0 %all_gather.20 = bf16[1024,384]{1,0:T(8,128)(2,1)S(1)} all-gather(bf16[16,384]{1,0:T(8,128)(2,1)S(1)} %fusion.29), channel_id=1, replica_groups=mesh['prow'=4,'pcol'=64] {'pcol'}, dimensions={0}, use_global_device_ids=true | all-gather | bytes 798720 | tf_op jit(solution)/shard_map/while/body/eval_jaxpr/all_gather | solution.py:12
  1723.9 54.0 %all_gather.21 = bf16[1024,384]{1,0:T(8,128)(2,1)S(1)} all-gather(bf16[16,384]{1,0:T(8,128)(2,1)S(1)} %get-tuple-element.425), channel_id=1, replica_groups=mesh['prow'=4,'pcol'=64] {'pcol'}, dimensions={0}, use_global_device_ids=true | all-gather | bytes 798720 | tf_op jit(solution)/shard_map/while/body/eval_jaxpr/all_gather | solution.py:21
  1780.2 76.2 %while.51 = (s32[]{:T(128)}, f32[64,384]{1,0:T(8,128)S(1)}, s32[]{:T(128)}, bf16[48,64,1024]{2,1,0:T(8,128)(2,1)}, s32[48]{0:T(128)S(1)}, /*index=5*/bf16[12,102...) while((s32[]{:T(128)}, f32[64,384]{1,0:T(8,128)S(1)}, s32[]{:T(128)}, ...), condition=%wide.region_4.4_spmd, body=%wide.region_3.3_spmd.sunk | while | flops 50356232 | bytes 1114301 | solution.py:58
  1875.0 54.0 %all_gather.20 = bf16[1024,384]{1,0:T(8,128)(2,1)S(1)} all-gather(bf16[16,384]{1,0:T(8,128)(2,1)S(1)} %fusion.29), channel_id=1, replica_groups=mesh['prow'=4,'pcol'=64] {'pcol'}, dimensions={0}, use_global_device_ids=true | all-gather | bytes 798720 | tf_op jit(solution)/shard_map/while/body/eval_jaxpr/all_gather | solution.py:12
  1948.7 54.0 %all_gather.21 = bf16[1024,384]{1,0:T(8,128)(2,1)S(1)} all-gather(bf16[16,384]{1,0:T(8,128)(2,1)S(1)} %get-tuple-element.425), channel_id=1, replica_groups=mesh['prow'=4,'pcol'=64] {'pcol'}, dimensions={0}, use_global_device_ids=true | all-gather | bytes 798720 | tf_op jit(solution)/shard_map/while/body/eval_jaxpr/all_gather | solution.py:21
  2003.8 69.9 %while.50 = (s32[]{:T(128)}, f32[64,384]{1,0:T(8,128)S(1)}, s32[]{:T(128)}, bf16[48,64,1024]{2,1,0:T(8,128)(2,1)}, s32[48]{0:T(128)S(1)}, /*index=5*/bf16[12,102...) while((s32[]{:T(128)}, f32[64,384]{1,0:T(8,128)S(1)}, s32[]{:T(128)}, ...), condition=%wide.region_9.10_spmd, body=%wide.region_8.9_spmd.sunk | while | flops 50356232 | bytes 1114301 | solution.py:58
  2092.2 54.1 %all_gather.17 = bf16[1024,384]{1,0:T(8,128)(2,1)S(1)} all-gather(bf16[16,384]{1,0:T(8,128)(2,1)S(1)} %fusion.15), channel_id=1, replica_groups=mesh['prow'=4,'pcol'=64] {'pcol'}, dimensions={0}, use_global_device_ids=true | all-gather | bytes 798720 | tf_op jit(solution)/shard_map/all_gather | solution.py:12
  (294 shorter events, 977.1 us)
Async XLA Ops:
  14.2 27.9 %reduce-scatter.9.cloned.1.call-start = ((), (), s32[]{:S(2)}) async-start(), calls=%async_computation.6 | async-start | bytes 122880 | tf_op jit(solution)/shard_map/while/body/eval_jaxpr/reduce_scatter | solution.py:8
  17.4 98.5 %reduce-scatter.11.cloned.1.call-start = ((), (), s32[]{:S(2)}) async-start(), calls=%async_computation.7 | async-start | bytes 122880 | tf_op jit(solution)/shard_map/while/body/eval_jaxpr/reduce_scatter | solution.py:15
  171.6 20.4 reduce-scatter.9.cloned.1.call-start
  174.8 91.1 %reduce-scatter.11.cloned.1.call-start = ((), (), s32[]{:S(2)}) async-start(), calls=%async_computation.7 | async-start | bytes 122880 | tf_op jit(solution)/shard_map/while/body/eval_jaxpr/reduce_scatter | solution.py:15
  321.6 37.0 %reduce-scatter.9.cloned.1.call-start = ((), (), s32[]{:S(2)}) async-start(), calls=%async_computation.6 | async-start | bytes 122880 | tf_op jit(solution)/shard_map/while/body/eval_jaxpr/reduce_scatter | solution.py:8
  341.4 91.0 %reduce-scatter.11.cloned.1.call-start = ((), (), s32[]{:S(2)}) async-start(), calls=%async_computation.7 | async-start | bytes 122880 | tf_op jit(solution)/shard_map/while/body/eval_jaxpr/reduce_scatter | solution.py:15
  488.2 37.0 %reduce-scatter.9.cloned.1.call-start = ((), (), s32[]{:S(2)}) async-start(), calls=%async_computation.6 | async-start | bytes 122880 | tf_op jit(solution)/shard_map/while/body/eval_jaxpr/reduce_scatter | solution.py:8
  508.0 91.0 %reduce-scatter.11.cloned.1.call-start = ((), (), s32[]{:S(2)}) async-start(), calls=%async_computation.7 | async-start | bytes 122880 | tf_op jit(solution)/shard_map/while/body/eval_jaxpr/reduce_scatter | solution.py:15
  654.7 45.4 %reduce-scatter.9.cloned.1.call-start = ((), (), s32[]{:S(2)}) async-start(), calls=%async_computation.6 | async-start | bytes 122880 | tf_op jit(solution)/shard_map/while/body/eval_jaxpr/reduce_scatter | solution.py:8
  682.9 91.0 %reduce-scatter.11.cloned.1.call-start = ((), (), s32[]{:S(2)}) async-start(), calls=%async_computation.7 | async-start | bytes 122880 | tf_op jit(solution)/shard_map/while/body/eval_jaxpr/reduce_scatter | solution.py:15
  829.6 45.4 %reduce-scatter.9.cloned.1.call-start = ((), (), s32[]{:S(2)}) async-start(), calls=%async_computation.6 | async-start | bytes 122880 | tf_op jit(solution)/shard_map/while/body/eval_jaxpr/reduce_scatter | solution.py:8
  857.8 91.0 %reduce-scatter.11.cloned.1.call-start = ((), (), s32[]{:S(2)}) async-start(), calls=%async_computation.7 | async-start | bytes 122880 | tf_op jit(solution)/shard_map/while/body/eval_jaxpr/reduce_scatter | solution.py:15
  1004.5 62.0 %reduce-scatter.9.cloned.1.call-start = ((), (), s32[]{:S(2)}) async-start(), calls=%async_computation.6 | async-start | bytes 122880 | tf_op jit(solution)/shard_map/while/body/eval_jaxpr/reduce_scatter | solution.py:8
  1049.3 91.0 %reduce-scatter.11.cloned.1.call-start = ((), (), s32[]{:S(2)}) async-start(), calls=%async_computation.7 | async-start | bytes 122880 | tf_op jit(solution)/shard_map/while/body/eval_jaxpr/reduce_scatter | solution.py:15
  1196.0 53.7 %reduce-scatter.9.cloned.1.call-start = ((), (), s32[]{:S(2)}) async-start(), calls=%async_computation.6 | async-start | bytes 122880 | tf_op jit(solution)/shard_map/while/body/eval_jaxpr/reduce_scatter | solution.py:8
  1232.5 91.1 %reduce-scatter.11.cloned.1.call-start = ((), (), s32[]{:S(2)}) async-start(), calls=%async_computation.7 | async-start | bytes 122880 | tf_op jit(solution)/shard_map/while/body/eval_jaxpr/reduce_scatter | solution.py:15
  1379.3 70.3 %reduce-scatter.9.cloned.1.call-start = ((), (), s32[]{:S(2)}) async-start(), calls=%async_computation.6 | async-start | bytes 122880 | tf_op jit(solution)/shard_map/while/body/eval_jaxpr/reduce_scatter | solution.py:8
  1432.4 91.0 %reduce-scatter.11.cloned.1.call-start = ((), (), s32[]{:S(2)}) async-start(), calls=%async_computation.7 | async-start | bytes 122880 | tf_op jit(solution)/shard_map/while/body/eval_jaxpr/reduce_scatter | solution.py:15
  1579.1 70.4 %reduce-scatter.9.cloned.1.call-start = ((), (), s32[]{:S(2)}) async-start(), calls=%async_computation.6 | async-start | bytes 122880 | tf_op jit(solution)/shard_map/while/body/eval_jaxpr/reduce_scatter | solution.py:8
  1632.2 91.0 %reduce-scatter.11.cloned.1.call-start = ((), (), s32[]{:S(2)}) async-start(), calls=%async_computation.7 | async-start | bytes 122880 | tf_op jit(solution)/shard_map/while/body/eval_jaxpr/reduce_scatter | solution.py:15
  1778.9 95.3 %reduce-scatter.9.cloned.1.call-start = ((), (), s32[]{:S(2)}) async-start(), calls=%async_computation.6 | async-start | bytes 122880 | tf_op jit(solution)/shard_map/while/body/eval_jaxpr/reduce_scatter | solution.py:8
  1857.0 91.0 %reduce-scatter.11.cloned.1.call-start = ((), (), s32[]{:S(2)}) async-start(), calls=%async_computation.7 | async-start | bytes 122880 | tf_op jit(solution)/shard_map/while/body/eval_jaxpr/reduce_scatter | solution.py:15
  2003.8 87.7 %reduce-scatter.5.cloned.1.call-start = ((), (), s32[]{:S(2)}) async-start(), calls=%async_computation.4 | async-start | bytes 122880 | tf_op jit(solution)/shard_map/reduce_scatter | solution.py:8
  2074.4 89.9 %reduce-scatter.7.cloned.1.call-start = ((), (), s32[]{:S(2)}) async-start(), calls=%async_computation.5 | async-start | bytes 122880 | tf_op jit(solution)/shard_map/reduce_scatter | solution.py:15
  (13 other events, 168.2 us)
Sparse Core Ops, SparseCore 0:
  17.6 24.4 reduce-scatter.8
  98.8 17.0 reduce-scatter.10
  175.0 17.0 reduce-scatter.8
  248.8 17.0 reduce-scatter.10
  341.5 17.0 reduce-scatter.8
  415.3 17.0 reduce-scatter.10
  508.1 17.0 reduce-scatter.8
  581.9 17.0 reduce-scatter.10
  683.0 17.0 reduce-scatter.8
  756.8 17.0 reduce-scatter.10
  857.9 17.0 reduce-scatter.8
  931.7 17.0 reduce-scatter.10
  1049.4 17.0 reduce-scatter.8
  1123.2 17.0 reduce-scatter.10
  1232.6 17.1 reduce-scatter.8
  1306.4 17.0 reduce-scatter.10
  1432.5 17.0 reduce-scatter.8
  1506.3 17.0 reduce-scatter.10
  1632.3 17.0 reduce-scatter.8
  1706.1 17.0 reduce-scatter.10
  1857.1 17.0 reduce-scatter.8
  1930.9 17.0 reduce-scatter.10
Sparse Core Ops, SparseCore 1:
  2074.4 17.0 reduce-scatter.4
  2147.3 16.9 reduce-scatter.6
where the time goes:
time: 2180 us; the launch traced here: 2170 us
  blocking collectives  1240 us (57%)
  waiting for transfers between devices  420 us (19%)
  loops' own time  318 us (15%)
  matrix products  91.3 us (4%)
  local copies, waits for them, and re-layouts  68.5 us (3%)
    all_gather x12, blocking collectives, finish_block(): lax.all_gather(residual, 'pcol', axis=0, tiled=True)  648 us
    all_gather x11, blocking collectives, spread_block(): return lax.all_gather(solved, 'pcol', axis=0, tiled=True)  594 us
    another operation x12, loops' own time, row_update(): lax.fori_loop(row_begin[current], row_end[current], accumulate, jnp.zeros...  317 us
    reduce_scatter x12, waiting for transfers between devices, finish_block(): lax.psum_scatter(partial_value, 'prow', scatter_dimension=0, tiled=True)  213 us
    reduce_scatter x12, waiting for transfers between devices, finish_block(): lax.psum_scatter(inverse_image, 'prow', scatter_dimension=0, tiled=True)  207 us
    dot_general x48, matrix products, accumulate(): return running + jnp.dot(matrix, source, preferred_element_type=jnp.float32)  70.7 us
  transfers between devices with their start and end apart: 24, of which 24 were waited for; matrix products, arithmetic and copies ran while one was open for 0% of the time, Pallas kernels for 0%

commit v1 on v0

v1 whole, which is shorter than its diff:
```python
import jax
import jax.numpy as jnp
from jax import lax
from jax.experimental import pallas as pl
from jax.experimental.pallas import tpu as pltpu
from jax.sharding import Mesh, PartitionSpec as P

ROWS, CHIPS, CORES = "prow", "chip", "core"


def spread(copies):
    received = lax.all_to_all(copies, CHIPS, 0, 0, tiled=True)
    return lax.all_gather(received, CORES, axis=0)


def interleave(gathered, whole):
    cores, chips, rows, _ = gathered.shape
    parts = whole.shape[0] // (cores * chips * 16)
    span = cores * chips * 16

    def place(chip, carry):
        for core in range(cores):
            for part in range(parts):
                first = pl.multiple_of(part * span + (chip * cores + core) * 16, 16)
                whole[pl.ds(first, 16), :] = gathered[core, chip, pl.ds(part * 16, 16), :]
        return carry

    lax.fori_loop(0, chips, place, 0, unroll=4)


def product(matrix, whole):
    span = matrix.shape[-1]
    total = None
    for part in range(matrix.shape[0]):
        term = jnp.dot(
            matrix[part], whole[pl.ds(part * span, span), :], preferred_element_type=jnp.float32
        )
        total = term if total is None else total + term
    return total


def copy_out(value, copies):
    for chip in range(copies.shape[0]):
        copies[chip] = value


def solve_kernel(gathered, inverse, copies, piece, whole, matrix, sem):
    load = pltpu.make_async_copy(inverse, matrix, sem)
    load.start()
    interleave(gathered, whole)
    load.wait()
    value = product(matrix, whole).astype(jnp.bfloat16)
    piece[...] = value
    copy_out(value, copies)


def residual_kernel(slots, gathered, factor, rhs, earlier, copies, whole, matrix, total, sem):
    last = slots.shape[0] - 1
    slot = slots[last]

    @pl.when(slot >= 0)
    def _():
        pltpu.make_async_copy(factor.at[:, slot], matrix, sem).start()

    interleave(gathered, whole)
    total[...] = earlier[...]

    @pl.when(slot >= 0)
    def _():
        pltpu.make_async_copy(factor.at[:, slot], matrix, sem).wait()
        total[...] += product(matrix, whole)

    copy_out((rhs[...].astype(jnp.float32) - total[...]).astype(jnp.bfloat16), copies)


def update_kernel(slots, factor, *refs):
    count = len(refs) - 5
    sources = refs[:count]
    total, wholes, matrices, sems, factor_sems = refs[count:]
    for column in range(count):

        @pl.when(slots[column] >= 0)
        def _(column=column):
            pltpu.make_async_copy(
                factor.at[:, slots[column]], matrices.at[column], factor_sems.at[column]
            ).start()
            pltpu.make_async_copy(sources[column], wholes.at[column], sems.at[column]).start()

    total[...] = jnp.zeros_like(total)

    def add(column, carry):
        slot = slots[column]

        @pl.when(slot >= 0)
        def _():
            pltpu.make_async_copy(
                factor.at[:, slot], matrices.at[column], factor_sems.at[column]
            ).wait()
            pltpu.make_async_copy(sources[0], wholes.at[column], sems.at[column]).wait()
            total[...] += product(matrices.at[column], wholes.at[column])

        return carry

    lax.fori_loop(0, count, add, 0)


def vmem():
    return pl.BlockSpec(memory_space=pltpu.VMEM)


def smem():
    return pl.BlockSpec(memory_space=pltpu.SMEM)


def anywhere():
    return pl.BlockSpec(memory_space=pl.ANY)


LIMIT = pltpu.CompilerParams(vmem_limit_bytes=32 * 1024 * 1024)


def solve(gathered, inverse):
    cores, chips, rows, columns = gathered.shape
    parts, _, span = inverse.shape
    return pl.pallas_call(
        solve_kernel,
        out_shape=(
            jax.ShapeDtypeStruct((chips, rows, columns), jnp.bfloat16),
            jax.ShapeDtypeStruct((rows, columns), jnp.bfloat16),
        ),
        in_specs=[vmem(), anywhere()],
        out_specs=(vmem(), vmem()),
        scratch_shapes=[
            pltpu.VMEM((parts * span, columns), jnp.bfloat16),
            pltpu.VMEM(inverse.shape, jnp.bfloat16),
            pltpu.SemaphoreType.DMA,
        ],
        compiler_params=LIMIT,
        name="solve",
    )(gathered, inverse)


def residual(slots, gathered, factor, rhs, earlier):
    cores, chips, rows, columns = gathered.shape
    parts, _, _, span = factor.shape
    return pl.pallas_call(
        residual_kernel,
        out_shape=(
            jax.ShapeDtypeStruct((chips, rows, columns), jnp.bfloat16),
            jax.ShapeDtypeStruct((parts * span, columns), jnp.bfloat16),
        ),
        in_specs=[smem(), vmem(), anywhere(), vmem(), vmem()],
        out_specs=(vmem(), vmem()),
        scratch_shapes=[
            pltpu.VMEM((parts, rows, span), jnp.bfloat16),
            pltpu.VMEM((rows, columns), jnp.float32),
            pltpu.SemaphoreType.DMA,
        ],
        compiler_params=LIMIT,
        name="residual",
    )(slots, gathered, factor, rhs, earlier)


def update(slots, factor, sources):
    parts, _, rows, span = factor.shape
    count = len(sources)
    columns = sources[0].shape[1]
    return pl.pallas_call(
        update_kernel,
        out_shape=jax.ShapeDtypeStruct((rows, columns), jnp.float32),
        in_specs=[smem(), anywhere()] + [anywhere()] * count,
        out_specs=vmem(),
        scratch_shapes=[
            pltpu.VMEM((count, parts * span, columns), jnp.bfloat16),
            pltpu.VMEM((count, parts, rows, span), jnp.bfloat16),
            pltpu.SemaphoreType.DMA((count,)),
            pltpu.SemaphoreType.DMA((count,)),
        ],
        compiler_params=LIMIT,
        cost_estimate=pl.CostEstimate(
            flops=count * 2 * rows * parts * span * 256,
            bytes_accessed=count * parts * span * (rows + 128) * 2,
            transcendentals=0,
        ),
        name="update",
    )(slots, factor, *sources)


def shards(rhs, factor_blocks, diag_inverses, block_index):
    blocks, piece_rows, total_columns = rhs.shape
    entries, parts = factor_blocks.shape[:2]
    span = factor_blocks.shape[-1]
    rows = parts * piece_rows
    columns = total_columns // parts
    chips = span // (piece_rows * 2)
    factor = factor_blocks.reshape(entries, rows, span)
    inverse = diag_inverses.reshape(blocks, rows, span)
    block_rows, block_cols = block_index[:, 0], block_index[:, 1]
    numbers = jnp.arange(blocks, dtype=jnp.int32)
    row_begin = jnp.sum((block_rows[None, :] < numbers[:, None]).astype(jnp.int32), axis=1)
    match = (block_rows[None, None, :] == numbers[:, None, None]) & (
        block_cols[None, None, :] == numbers[None, :, None]
    )
    places = jnp.arange(1, entries + 1, dtype=jnp.int32)
    table = jnp.sum(jnp.where(match, places, 0), axis=2) - 1

    split = rhs.reshape(blocks, piece_rows, parts, columns).transpose(2, 0, 1, 3)
    split = lax.all_to_all(split, ROWS, 0, 0, tiled=True)

    def rhs_of(current):
        return split[:, current].reshape(rows, columns)

    def gather_row(current, after):
        first = jnp.minimum(row_begin[current], entries - current)
        slots = table[current, :current]
        slots = jnp.where(slots >= 0, slots - first, -1)
        slab = lax.dynamic_slice(factor, (first, 0, 0), (current, rows, span))
        if after is not None:
            slab, after = lax.optimization_barrier((slab, after))
        return slots, lax.all_gather(slab, ROWS, axis=0)

    def gather_inverse(current, after):
        slab = inverse[current]
        if after is not None:
            slab, after = lax.optimization_barrier((slab, after))
        return lax.all_gather(slab, ROWS, axis=0)

    ahead = 3
    inverses = {0: gather_inverse(0, None)}
    factors = {}
    for current in range(1, ahead):
        factors[current] = gather_row(current, None)
        inverses[current] = gather_inverse(current, None)
    copies = jnp.broadcast_to(rhs_of(0)[None], (chips, rows, columns))
    history, pieces = [], []
    for current in range(blocks):
        gathered = spread(copies)
        coming = current + ahead
        if coming < blocks:
            factors[coming] = gather_row(coming, gathered)
            inverses[coming] = gather_inverse(coming, gathered)
        copies, piece = solve(gathered, inverses[current])
        pieces.append(piece)
        if current + 1 == blocks:
            break
        slots, row_factor = factors[current + 1]
        if history:
            earlier = update(slots[:-1], row_factor, history)
        else:
            earlier = jnp.zeros((rows, columns), jnp.float32)
        gathered = spread(copies)
        copies, whole = residual(slots, gathered, row_factor, rhs_of(current + 1), earlier)
        history.append(whole)

    out = jnp.stack(pieces).reshape(blocks, parts, piece_rows, columns).transpose(1, 0, 2, 3)
    out = lax.all_to_all(out, ROWS, 0, 0, tiled=True)
    return out.transpose(1, 2, 0, 3).reshape(blocks, piece_rows, total_columns)


def solution(mesh):
    cores = 2
    across, along = mesh.shape["prow"], mesh.shape["pcol"]
    grid = Mesh(mesh.devices.reshape(across, along // cores, cores), (ROWS, CHIPS, CORES))
    column = (CHIPS, CORES)
    in_specs = (
        P(None, (ROWS, CHIPS, CORES), None),
        P(None, None, column, None, ROWS),
        P(None, None, column, None, ROWS),
        P(),
    )
    out_specs = P(None, (ROWS, CHIPS, CORES), None)
    return jax.shard_map(shards, mesh=grid, in_specs=in_specs, out_specs=out_specs, check_vma=False)
```

time: 2180 us -> 944 us (0.43)
  blocking collectives: 1240 us -> 359 us
  loops' own time: 318 us -> 0 us
  waiting for transfers between devices: 420 us -> 260 us
  starting transfers between devices: 0.58 us -> 118 us
  matrix products: 91.3 us -> 0 us
  local copies, waits for them, and re-layouts: 68.5 us -> 125 us
  Pallas kernels: 0 us -> 50 us
    all_gather x23 -> x36, blocking collectives: 1240 us -> 340 us  [the longest x23 198 us: spread(): return lax.all_gather(received, CORES, axis=0)]
    reduce_scatter x24 -> x0, waiting for transfers between devices: 419 us -> none  [the longest x12 213 us: finish_block(): lax.psum_scatter(partial_value, 'prow', scatter_dimension=0, tiled=True)]
    another operation x13 -> x0, loops' own time: 318 us -> none  [the longest x12 317 us: row_update(): lax.fori_loop(row_begin[current], row_end[current], accumulate, jnp.zeros...]
    all_to_all x0 -> x23, waiting for transfers between devices: none -> 259 us  [spread(): received = lax.all_to_all(copies, CHIPS, 0, 0, tiled=True)]
    all_to_all x0 -> x23, starting transfers between devices: none -> 117 us  [spread(): received = lax.all_to_all(copies, CHIPS, 0, 0, tiled=True)]
    unnamed x4 -> x181, local copies, waits for them, and re-layouts: 0.62 us -> 95.8 us
    dot_general x60 -> x0, matrix products: 91.3 us -> none  [the longest x48 70.7 us: accumulate(): return running + jnp.dot(matrix, source, preferred_element_type=jnp.float32)]
    pallas_call x0 -> x33, Pallas kernels: none -> 50 us  [the longest x10 22.9 us: update(): pl.pallas_call(update_kernel, out_shape=jax.ShapeDtypeStruct((rows, colum...]
  transfers between devices with their start and end apart: 24 -> 33, of which waited for: 24 -> 22; matrix products, arithmetic and copies ran while one was open for 0% -> 3% of each run, Pallas kernels for 0% -> 5%
where the time goes in v1:
time: 944 us; the launch traced here: 935 us
  blocking collectives  359 us (38%)
  waiting for transfers between devices  260 us (28%)
  local copies, waits for them, and re-layouts  125 us (13%)
  starting transfers between devices  118 us (12%)
  Pallas kernels  50 us (5%)
  between operations  22.9 us (2%)
    all_to_all x23, waiting for transfers between devices, spread(): received = lax.all_to_all(copies, CHIPS, 0, 0, tiled=True)  259 us
    all_gather x23, blocking collectives, spread(): return lax.all_gather(received, CORES, axis=0)  198 us
    all_gather x12, blocking collectives, gather_inverse(): return lax.all_gather(slab, ROWS, axis=0)  131 us
    all_to_all x23, starting transfers between devices, spread(): received = lax.all_to_all(copies, CHIPS, 0, 0, tiled=True)  117 us
    unnamed x181, local copies, waits for them, and re-layouts  95.8 us
    pallas_call x10, Pallas kernels, update(): pl.pallas_call(update_kernel, out_shape=jax.ShapeDtypeStruct((rows, colum...  22.9 us
    dynamic_slice x11, local copies, waits for them, and re-layouts, gather_row(): slab = lax.dynamic_slice(factor, (first, 0, 0), (current, rows, span))  22.4 us
  transfers between devices with their start and end apart: 33, of which 22 were waited for; matrix products, arithmetic and copies ran while one was open for 3% of the time, Pallas kernels for 5%

profile of v1, /device:TPU:1, one launch (start us, length us, event | category | flops | bytes accessed | tf_op | source)
XLA Modules:
  0.0 934.6 jit_solution(382768645324785105)
XLA Ops:
  36.1 12.0 %all-to-all-done.1 = bf16[32,64,96]{2,1,0:T(8,128)(2,1)S(1)} async-done(((bf16[32,64,96]{2,1,0:T(8,128)(2,1)}), bf16[32,64,96]{2,1,0:T(8,128)(2,1)S(1)}, u32[]{:S(2)}, u32[]{:S(2)}) %all-to-all-start.1) | async-done | bytes 393248 | tf_op jit(solution)/shard_map/all_to_all | solution.py:12
  56.5 11.9 %all_gather.269.inverse = bf16[4,64,1024]{2,1,0:T(8,128)(2,1)S(1)} all-gather(bf16[1,64,1024]{2,1,0:T(8,128)(2,1)} %bitcast.264), channel_id=1, replica_groups=mesh['prow'=4,'chip'=32,'core'=2] {'prow'}, dimensions={0}, use_global_device_ids=true | all-gather | bytes 655360 | tf_op jit(solution)/shard_map/all_gather | solution.py:226
  109.2 14.1 %all-to-all-done.3 = bf16[32,64,96]{2,1,0:T(8,128)(2,1)S(1)} async-done(((bf16[32,64,96]{2,1,0:T(8,128)(2,1)}), bf16[32,64,96]{2,1,0:T(8,128)(2,1)S(1)}, u32[]{:S(2)}, u32[]{:S(2)}) %all-to-all-start.3) | async-done | bytes 393248 | tf_op jit(solution)/shard_map/all_to_all | solution.py:12
  176.0 14.0 %all-to-all-done.5 = bf16[32,64,96]{2,1,0:T(8,128)(2,1)} async-done(((bf16[32,64,96]{2,1,0:T(8,128)(2,1)}), bf16[32,64,96]{2,1,0:T(8,128)(2,1)}, u32[]{:S(2)}, u32[]{:S(2)}) %all-to-all-start.5) | async-done | bytes 393248 | tf_op jit(solution)/shard_map/all_to_all | solution.py:12
  243.1 13.8 %all-to-all-done.7 = bf16[32,64,96]{2,1,0:T(8,128)(2,1)} async-done(((bf16[32,64,96]{2,1,0:T(8,128)(2,1)}), bf16[32,64,96]{2,1,0:T(8,128)(2,1)}, u32[]{:S(2)}, u32[]{:S(2)}) %all-to-all-start.7) | async-done | bytes 393248 | tf_op jit(solution)/shard_map/all_to_all | solution.py:12
  317.7 13.7 %all-to-all-done.9 = bf16[32,64,96]{2,1,0:T(8,128)(2,1)} async-done(((bf16[32,64,96]{2,1,0:T(8,128)(2,1)}), bf16[32,64,96]{2,1,0:T(8,128)(2,1)}, u32[]{:S(2)}, u32[]{:S(2)}) %all-to-all-start.9) | async-done | bytes 393248 | tf_op jit(solution)/shard_map/all_to_all | solution.py:12
  358.7 13.0 %all-to-all-done.10 = bf16[32,64,96]{2,1,0:T(8,128)(2,1)} async-done(((bf16[32,64,96]{2,1,0:T(8,128)(2,1)}), bf16[32,64,96]{2,1,0:T(8,128)(2,1)}, u32[]{:S(2)}, u32[]{:S(2)}) %all-to-all-start.10) | async-done | bytes 393248 | tf_op jit(solution)/shard_map/all_to_all | solution.py:12
  371.7 13.0 %all-gather.15 = bf16[64,64,96]{2,1,0:T(8,128)(2,1)} all-gather(bf16[32,64,96]{2,1,0:T(8,128)(2,1)} %all-to-all-done.10), channel_id=17, replica_groups=mesh['prow'=4,'chip'=32,'core'=2] {'core'}, dimensions={0}, use_global_device_ids=true | all-gather | bytes 1179648 | tf_op jit(solution)/shard_map/all_gather | solution.py:13
  400.4 13.8 %all-to-all-done.11 = bf16[32,64,96]{2,1,0:T(8,128)(2,1)} async-done(((bf16[32,64,96]{2,1,0:T(8,128)(2,1)}), bf16[32,64,96]{2,1,0:T(8,128)(2,1)}, u32[]{:S(2)}, u32[]{:S(2)}) %all-to-all-start.11) | async-done | bytes 393248 | tf_op jit(solution)/shard_map/all_to_all | solution.py:12
  441.1 13.0 %all-to-all-done.12 = bf16[32,64,96]{2,1,0:T(8,128)(2,1)} async-done(((bf16[32,64,96]{2,1,0:T(8,128)(2,1)}), bf16[32,64,96]{2,1,0:T(8,128)(2,1)}, u32[]{:S(2)}, u32[]{:S(2)}) %all-to-all-start.12) | async-done | bytes 393248 | tf_op jit(solution)/shard_map/all_to_all | solution.py:12
  454.2 13.0 %all-gather.19 = bf16[64,64,96]{2,1,0:T(8,128)(2,1)} all-gather(bf16[32,64,96]{2,1,0:T(8,128)(2,1)} %all-to-all-done.12), channel_id=21, replica_groups=mesh['prow'=4,'chip'=32,'core'=2] {'core'}, dimensions={0}, use_global_device_ids=true | all-gather | bytes 1179648 | tf_op jit(solution)/shard_map/all_gather | solution.py:13
  484.6 13.7 %all-to-all-done.13 = bf16[32,64,96]{2,1,0:T(8,128)(2,1)} async-done(((bf16[32,64,96]{2,1,0:T(8,128)(2,1)}), bf16[32,64,96]{2,1,0:T(8,128)(2,1)}, u32[]{:S(2)}, u32[]{:S(2)}) %all-to-all-start.13) | async-done | bytes 393248 | tf_op jit(solution)/shard_map/all_to_all | solution.py:12
  525.3 13.0 %all-to-all-done.14 = bf16[32,64,96]{2,1,0:T(8,128)(2,1)} async-done(((bf16[32,64,96]{2,1,0:T(8,128)(2,1)}), bf16[32,64,96]{2,1,0:T(8,128)(2,1)}, u32[]{:S(2)}, u32[]{:S(2)}) %all-to-all-start.14) | async-done | bytes 393248 | tf_op jit(solution)/shard_map/all_to_all | solution.py:12
  538.3 13.0 %all-gather.23 = bf16[64,64,96]{2,1,0:T(8,128)(2,1)} all-gather(bf16[32,64,96]{2,1,0:T(8,128)(2,1)} %all-to-all-done.14), channel_id=25, replica_groups=mesh['prow'=4,'chip'=32,'core'=2] {'core'}, dimensions={0}, use_global_device_ids=true | all-gather | bytes 1179648 | tf_op jit(solution)/shard_map/all_gather | solution.py:13
  570.8 13.6 %all-to-all-done.15 = bf16[32,64,96]{2,1,0:T(8,128)(2,1)} async-done(((bf16[32,64,96]{2,1,0:T(8,128)(2,1)}), bf16[32,64,96]{2,1,0:T(8,128)(2,1)}, u32[]{:S(2)}, u32[]{:S(2)}) %all-to-all-start.15) | async-done | bytes 393248 | tf_op jit(solution)/shard_map/all_to_all | solution.py:12
  611.4 13.0 %all-to-all-done.16 = bf16[32,64,96]{2,1,0:T(8,128)(2,1)} async-done(((bf16[32,64,96]{2,1,0:T(8,128)(2,1)}), bf16[32,64,96]{2,1,0:T(8,128)(2,1)}, u32[]{:S(2)}, u32[]{:S(2)}) %all-to-all-start.16) | async-done | bytes 393248 | tf_op jit(solution)/shard_map/all_to_all | solution.py:12
  624.4 13.0 %all-gather.27 = bf16[64,64,96]{2,1,0:T(8,128)(2,1)} all-gather(bf16[32,64,96]{2,1,0:T(8,128)(2,1)} %all-to-all-done.16), channel_id=29, replica_groups=mesh['prow'=4,'chip'=32,'core'=2] {'core'}, dimensions={0}, use_global_device_ids=true | all-gather | bytes 1179648 | tf_op jit(solution)/shard_map/all_gather | solution.py:13
  658.8 13.4 %all-to-all-done.17 = bf16[32,64,96]{2,1,0:T(8,128)(2,1)} async-done(((bf16[32,64,96]{2,1,0:T(8,128)(2,1)}), bf16[32,64,96]{2,1,0:T(8,128)(2,1)}, u32[]{:S(2)}, u32[]{:S(2)}) %all-to-all-start.17) | async-done | bytes 393248 | tf_op jit(solution)/shard_map/all_to_all | solution.py:12
  699.5 13.0 %all-to-all-done.18 = bf16[32,64,96]{2,1,0:T(8,128)(2,1)} async-done(((bf16[32,64,96]{2,1,0:T(8,128)(2,1)}), bf16[32,64,96]{2,1,0:T(8,128)(2,1)}, u32[]{:S(2)}, u32[]{:S(2)}) %all-to-all-start.18) | async-done | bytes 393248 | tf_op jit(solution)/shard_map/all_to_all | solution.py:12
  712.5 13.0 %all-gather.31 = bf16[64,64,96]{2,1,0:T(8,128)(2,1)} all-gather(bf16[32,64,96]{2,1,0:T(8,128)(2,1)} %all-to-all-done.18), channel_id=33, replica_groups=mesh['prow'=4,'chip'=32,'core'=2] {'core'}, dimensions={0}, use_global_device_ids=true | all-gather | bytes 1179648 | tf_op jit(solution)/shard_map/all_gather | solution.py:13
  744.3 11.9 %all-gather.34 = bf16[256,1024]{1,0:T(8,128)(2,1)} all-gather(bf16[64,1024]{1,0:T(8,128)(2,1)} %bitcast.255), channel_id=36, replica_groups=mesh['prow'=4,'chip'=32,'core'=2] {'prow'}, dimensions={0}, use_global_device_ids=true | all-gather | bytes 655360 | tf_op jit(solution)/shard_map/all_gather | solution.py:226
  772.9 16.5 %all-to-all-done.20 = bf16[32,64,96]{2,1,0:T(8,128)(2,1)} async-done(((bf16[32,64,96]{2,1,0:T(8,128)(2,1)}), bf16[32,64,96]{2,1,0:T(8,128)(2,1)}, u32[]{:S(2)}, u32[]{:S(2)}) %all-to-all-start.20) | async-done | bytes 393248 | tf_op jit(solution)/shard_map/all_to_all | solution.py:12
  820.1 12.3 %all-gather.38 = bf16[256,1024]{1,0:T(8,128)(2,1)} all-gather(bf16[64,1024]{1,0:T(8,128)(2,1)} %bitcast.254), channel_id=40, replica_groups=mesh['prow'=4,'chip'=32,'core'=2] {'prow'}, dimensions={0}, use_global_device_ids=true | all-gather | bytes 655360 | tf_op jit(solution)/shard_map/all_gather | solution.py:226
  851.7 13.5 %all-to-all-done.22 = bf16[32,64,96]{2,1,0:T(8,128)(2,1)} async-done(((bf16[32,64,96]{2,1,0:T(8,128)(2,1)}), bf16[32,64,96]{2,1,0:T(8,128)(2,1)}, u32[]{:S(2)}, u32[]{:S(2)}) %all-to-all-start.22) | async-done | bytes 393248 | tf_op jit(solution)/shard_map/all_to_all | solution.py:12
  (361 shorter events, 593.5 us)
Async XLA Ops:
  6.5 137.5 %all-gather.54.cloned.1.call-start = ((), (), s32[]{:S(2)}) async-start(), calls=%async_computation.25 | async-start | bytes 1310720 | tf_op jit(solution)/shard_map/all_gather | solution.py:220
  22.5 25.6 %all-to-all-start.1 = ((bf16[32,64,96]{2,1,0:T(8,128)(2,1)}), bf16[32,64,96]{2,1,0:T(8,128)(2,1)S(1)}, u32[]{:S(2)}, u32[]{:S(2)}) async-start(bf16[32,64,96]{2,1,0:T(8,128)(2,1)} %broadcast_in_dim.64), calls=%async_computation.1 | async-start | bytes 1048576 | tf_op jit(solution)/shard_map/all_to_all | solution.py:12
  33.6 177.4 %all-gather.56.cloned.1.call-start = ((), (), s32[]{:S(2)}) async-start(), calls=%async_computation.26 | async-start | bytes 1966080 | tf_op jit(solution)/shard_map/all_gather | solution.py:220
  97.2 26.1 %all-to-all-start.3 = ((bf16[32,64,96]{2,1,0:T(8,128)(2,1)}), bf16[32,64,96]{2,1,0:T(8,128)(2,1)S(1)}, u32[]{:S(2)}, u32[]{:S(2)}) async-start(bf16[32,64,96]{2,1,0:T(8,128)(2,1)} %get-tuple-element.69), calls=%async_computation.3 | async-start | bytes 1048576 | tf_op jit(solution)/shard_map/all_to_all | solution.py:12
  106.7 177.4 %all-gather.58.cloned.1.call-start = ((), (), s32[]{:S(2)}) async-start(), calls=%async_computation.27 | async-start | bytes 2621440 | tf_op jit(solution)/shard_map/all_gather | solution.py:220
  168.8 21.2 %all-to-all-start.5 = ((bf16[32,64,96]{2,1,0:T(8,128)(2,1)}), bf16[32,64,96]{2,1,0:T(8,128)(2,1)}, u32[]{:S(2)}, u32[]{:S(2)}) async-start(bf16[32,64,96]{2,1,0:T(8,128)(2,1)} %copy-done.68), calls=%async_computation.5 | async-start | bytes 1048576 | tf_op jit(solution)/shard_map/all_to_all | solution.py:12
  173.4 211.3 %all-gather.60.cloned.1.call-start = ((), (), s32[]{:S(2)}) async-start(), calls=%async_computation.28 | async-start | bytes 3276800 | tf_op jit(solution)/shard_map/all_gather | solution.py:220
  235.7 21.3 %all-to-all-start.7 = ((bf16[32,64,96]{2,1,0:T(8,128)(2,1)}), bf16[32,64,96]{2,1,0:T(8,128)(2,1)}, u32[]{:S(2)}, u32[]{:S(2)}) async-start(bf16[32,64,96]{2,1,0:T(8,128)(2,1)} %copy-done.69), calls=%async_computation.7 | async-start | bytes 1048576 | tf_op jit(solution)/shard_map/all_to_all | solution.py:12
  240.3 226.9 %all-gather.62.cloned.1.call-start = ((), (), s32[]{:S(2)}) async-start(), calls=%async_computation.29 | async-start | bytes 3932160 | tf_op jit(solution)/shard_map/all_gather | solution.py:220
  310.1 21.3 %all-to-all-start.9 = ((bf16[32,64,96]{2,1,0:T(8,128)(2,1)}), bf16[32,64,96]{2,1,0:T(8,128)(2,1)}, u32[]{:S(2)}, u32[]{:S(2)}) async-start(bf16[32,64,96]{2,1,0:T(8,128)(2,1)} %copy-done.70), calls=%async_computation.9 | async-start | bytes 1048576 | tf_op jit(solution)/shard_map/all_to_all | solution.py:12
  314.7 236.6 %all-gather.64.cloned.1.call-start = ((), (), s32[]{:S(2)}) async-start(), calls=%async_computation.30 | async-start | bytes 4587520 | tf_op jit(solution)/shard_map/all_gather | solution.py:220
  392.8 21.4 %all-to-all-start.11 = ((bf16[32,64,96]{2,1,0:T(8,128)(2,1)}), bf16[32,64,96]{2,1,0:T(8,128)(2,1)}, u32[]{:S(2)}, u32[]{:S(2)}) async-start(bf16[32,64,96]{2,1,0:T(8,128)(2,1)} %copy-done.71), calls=%async_computation.11 | async-start | bytes 1048576 | tf_op jit(solution)/shard_map/all_to_all | solution.py:12
  397.4 240.0 %all-gather.66.cloned.1.call-start = ((), (), s32[]{:S(2)}) async-start(), calls=%async_computation.31 | async-start | bytes 5242880 | tf_op jit(solution)/shard_map/all_gather | solution.py:220
  476.9 21.4 %all-to-all-start.13 = ((bf16[32,64,96]{2,1,0:T(8,128)(2,1)}), bf16[32,64,96]{2,1,0:T(8,128)(2,1)}, u32[]{:S(2)}, u32[]{:S(2)}) async-start(bf16[32,64,96]{2,1,0:T(8,128)(2,1)} %copy-done.72), calls=%async_computation.13 | async-start | bytes 1048576 | tf_op jit(solution)/shard_map/all_to_all | solution.py:12
  481.5 244.0 %all-gather.68.cloned.1.call-start = ((), (), s32[]{:S(2)}) async-start(), calls=%async_computation.32 | async-start | bytes 5898240 | tf_op jit(solution)/shard_map/all_gather | solution.py:220
  563.0 21.4 %all-to-all-start.15 = ((bf16[32,64,96]{2,1,0:T(8,128)(2,1)}), bf16[32,64,96]{2,1,0:T(8,128)(2,1)}, u32[]{:S(2)}, u32[]{:S(2)}) async-start(bf16[32,64,96]{2,1,0:T(8,128)(2,1)} %copy-done.73), calls=%async_computation.15 | async-start | bytes 1048576 | tf_op jit(solution)/shard_map/all_to_all | solution.py:12
  567.6 231.0 %all-gather.70.cloned.1.call-start = ((), (), s32[]{:S(2)}) async-start(), calls=%async_computation.33 | async-start | bytes 6553600 | tf_op jit(solution)/shard_map/all_gather | solution.py:220
  650.9 21.4 %all-to-all-start.17 = ((bf16[32,64,96]{2,1,0:T(8,128)(2,1)}), bf16[32,64,96]{2,1,0:T(8,128)(2,1)}, u32[]{:S(2)}, u32[]{:S(2)}) async-start(bf16[32,64,96]{2,1,0:T(8,128)(2,1)} %copy-done.67), calls=%async_computation.17 | async-start | bytes 1048576 | tf_op jit(solution)/shard_map/all_to_all | solution.py:12
  655.5 219.0 %all-gather.72.cloned.1.call-start = ((), (), s32[]{:S(2)}) async-start(), calls=%async_computation.34 | async-start | bytes 7208960 | tf_op jit(solution)/shard_map/all_gather | solution.py:220
  739.7 21.4 %all-to-all-start.19 = ((bf16[32,64,96]{2,1,0:T(8,128)(2,1)}), bf16[32,64,96]{2,1,0:T(8,128)(2,1)}, u32[]{:S(2)}, u32[]{:S(2)}) async-start(bf16[32,64,96]{2,1,0:T(8,128)(2,1)} %copy-done.82), calls=%async_computation.19 | async-start | bytes 1048576 | tf_op jit(solution)/shard_map/all_to_all | solution.py:12
  767.9 21.4 %all-to-all-start.20 = ((bf16[32,64,96]{2,1,0:T(8,128)(2,1)}), bf16[32,64,96]{2,1,0:T(8,128)(2,1)}, u32[]{:S(2)}, u32[]{:S(2)}) async-start(bf16[32,64,96]{2,1,0:T(8,128)(2,1)} %copy-done.83), calls=%async_computation.20 | async-start | bytes 1048576 | tf_op jit(solution)/shard_map/all_to_all | solution.py:12
  815.4 21.2 %all-to-all-start.21 = ((bf16[32,64,96]{2,1,0:T(8,128)(2,1)}), bf16[32,64,96]{2,1,0:T(8,128)(2,1)}, u32[]{:S(2)}, u32[]{:S(2)}) async-start(bf16[32,64,96]{2,1,0:T(8,128)(2,1)} %copy-done.76), calls=%async_computation.21 | async-start | bytes 1048576 | tf_op jit(solution)/shard_map/all_to_all | solution.py:12
  843.8 21.4 %all-to-all-start.22 = ((bf16[32,64,96]{2,1,0:T(8,128)(2,1)}), bf16[32,64,96]{2,1,0:T(8,128)(2,1)}, u32[]{:S(2)}, u32[]{:S(2)}) async-start(bf16[32,64,96]{2,1,0:T(8,128)(2,1)} %copy-done.66), calls=%async_computation.22 | async-start | bytes 1048576 | tf_op jit(solution)/shard_map/all_to_all | solution.py:12
  890.7 21.1 %all-to-all-start.23 = ((bf16[32,64,96]{2,1,0:T(8,128)(2,1)}), bf16[32,64,96]{2,1,0:T(8,128)(2,1)S(1)}, u32[]{:S(2)}, u32[]{:S(2)}) async-start(bf16[32,64,96]{2,1,0:T(8,128)(2,1)} %get-tuple-element.126), calls=%async_computation.23 | async-start | bytes 1048576 | tf_op jit(solution)/shard_map/all_to_all | solution.py:12
  (94 other events, 322.9 us)
Sparse Core Ops, SparseCore 0:
  10.6 29.4 all-gather.53
  54.8 25.1 all-gather.55
  127.8 28.3 all-gather.57
  194.6 33.3 all-gather.59
  266.1 37.4 all-gather.61
  340.6 41.6 all-gather.63
  423.1 46.1 all-gather.65
  507.2 50.4 all-gather.67
  593.3 54.7 all-gather.69
  681.2 58.8 all-gather.71

commit v2 on v0

v2 whole, which is shorter than its diff:
```python
import jax
import jax.numpy as jnp
from jax import lax
from jax.experimental import pallas as pl
from jax.experimental.pallas import tpu as pltpu
from jax.sharding import Mesh, PartitionSpec as P

ROWS, CHIPS, CORES = "prow", "chip", "core"
LANES = 128
CHUNK_ROWS = ((0, 1), (2, 3), (4, 5), (6, 7), (8, 9), (10, 11))
CHUNK_AFTER = (None, None, 0, 2, 4, 6)


def spread(copies):
    received = lax.all_to_all(copies, CHIPS, 0, 0, tiled=True)
    return lax.all_gather(received, CORES, axis=0)


def lane_of(shape):
    return lax.broadcasted_iota(jnp.int32, shape, 1)


def pack(value, parts):
    height = value.shape[0] // parts
    spare = LANES // parts
    last = value[(parts - 1) * height :]
    lane = lane_of(last.shape)
    packed = []
    for part in range(parts - 1):
        moved = pltpu.roll(last, LANES - spare - spare * part, 1)
        packed.append(
            jnp.where(lane < LANES - spare, value[part * height : (part + 1) * height], moved)
        )
    return jnp.concatenate(packed, axis=0).astype(jnp.bfloat16)


def copy_out(value, copies):
    for chip in range(copies.shape[0]):
        copies[chip] = value


def interleave(gathered, whole):
    cores, chips, height, _ = gathered.shape

    def place(chip, carry):
        for core in range(cores):
            first = pl.multiple_of((chip * cores + core) * 16, 16)
            for part in range(height // 16):
                whole[part, pl.ds(first, 16), :] = gathered[core, chip, pl.ds(part * 16, 16), :]
        return carry

    lax.fori_loop(0, chips, place, 0, unroll=8)


def raw_products(matrix, whole):
    parts = matrix.shape[0]
    last = matrix[parts - 1]
    return [
        jnp.dot(
            jnp.concatenate([matrix[part], last], axis=0),
            whole[part],
            preferred_element_type=jnp.float32,
        )
        for part in range(parts - 1)
    ]


def combine(raw):
    rows = raw[0].shape[0] // 2
    parts = len(raw) + 1
    spare = LANES // parts
    total = raw[0][:rows]
    for term in raw[1:]:
        total = total + term[:rows]
    lane = lane_of(total.shape)
    extra = pltpu.roll(raw[-1][rows:], spare * len(raw), 1)
    for part in reversed(range(len(raw) - 1)):
        moved = pltpu.roll(raw[part][rows:], spare * (part + 1), 1)
        extra = jnp.where(lane < spare * (part + 1), moved, extra)
    return total + extra


def widen(value, wide):
    wide[...] = jnp.zeros_like(wide)
    wide[:, pl.ds(0, value.shape[1])] = value
    return wide[...]


def start_entry(entry, chunks, spans, target, sem):
    for chunk, (low, high, offset) in zip(chunks, spans):

        @pl.when((entry >= low) & (entry < high))
        def _(chunk=chunk, low=low, high=high, offset=offset):
            place = jnp.clip(entry - low, 0, high - low - 1) + offset
            pltpu.make_async_copy(chunk.at[:, place], target, sem).start()


def wait_entry(chunks, target, sem):
    pltpu.make_async_copy(chunks[0].at[:, 0], target, sem).wait()


def first_kernel(rhs, copies, wide):
    parts, _, height, columns = rhs.shape
    value = rhs[:, 0].astype(jnp.float32).reshape(parts * height, columns)
    copy_out(pack(widen(value, wide), parts), copies)


def solve_kernel(current, place, gathered, chunk, *refs):
    if current:
        refs = refs[1:]
    copies, pieces, whole, matrix, sem = refs
    parts, _, height, columns = pieces.shape
    load = pltpu.make_async_copy(chunk.at[:, place], matrix, sem)
    load.start()
    interleave(gathered, whole)
    load.wait()
    value = combine(raw_products(matrix, whole))
    pieces[:, current] = value[:, :columns].astype(jnp.bfloat16).reshape(parts, height, columns)
    copy_out(pack(value, parts), copies)


def residual_kernel(current, spans, slots, gathered, rhs, *refs):
    count = len(spans)
    chunks, refs = refs[:count], refs[count:]
    parts, blocks, height, columns = rhs.shape
    keeps = current + 1 < blocks
    if current > 1:
        earlier, refs = refs[0], refs[1 + keeps :]
    copies, refs = refs[0], refs[1:]
    if keeps:
        history, refs = refs[0], refs[1:]
    whole, matrix, wide, total, sems = refs
    entry = slots[current - 1]
    start_entry(entry, chunks, spans, matrix, sems.at[0])
    interleave(gathered, whole)
    if keeps:
        keep = pltpu.make_async_copy(whole, history.at[current - 1], sems.at[1])
        keep.start()
    value = rhs[:, current].astype(jnp.float32).reshape(parts * height, columns)
    value = widen(value, wide)
    if current > 1:
        total[...] = earlier[...]
    else:
        total[...] = jnp.zeros_like(total)

    @pl.when(entry >= 0)
    def _():
        wait_entry(chunks, matrix, sems.at[0])
        total[...] += combine(raw_products(matrix, whole))

    copy_out(pack(value - total[...], parts), copies)
    if keeps:
        keep.wait()


def update_kernel(spans, slots, history, *refs):
    chunks, refs = refs[: len(spans)], refs[len(spans) :]
    result, wholes, matrices, total, history_sems, factor_sems = refs
    count = wholes.shape[0]
    for column in range(count):
        entry = slots[column]

        @pl.when(entry >= 0)
        def _(column=column):
            pltpu.make_async_copy(
                history.at[column], wholes.at[column], history_sems.at[column]
            ).start()

        start_entry(entry, chunks, spans, matrices.at[column], factor_sems.at[column])

    total[...] = jnp.zeros_like(total)

    def add(column, carry):
        @pl.when(slots[column] >= 0)
        def _():
            wait_entry(chunks, matrices.at[column], factor_sems.at[column])
            pltpu.make_async_copy(
                history.at[0], wholes.at[column], history_sems.at[column]
            ).wait()
            for part, term in enumerate(raw_products(matrices.at[column], wholes.at[column])):
                total[part] += term

        return carry

    lax.fori_loop(0, count, add, 0)
    result[...] = combine([total[part] for part in range(total.shape[0])])


def vmem():
    return pl.BlockSpec(memory_space=pltpu.VMEM)


def smem():
    return pl.BlockSpec(memory_space=pltpu.SMEM)


def anywhere():
    return pl.BlockSpec(memory_space=pl.ANY)


def in_vmem(array):
    return pltpu.with_memory_space_constraint(array, pltpu.VMEM)


def in_hbm(array):
    return pltpu.with_memory_space_constraint(array, pltpu.HBM)


LIMIT = pltpu.CompilerParams(vmem_limit_bytes=24 * 1024 * 1024)


def shards(rhs, factor_blocks, diag_inverses, block_index):
    blocks, height, total_columns = rhs.shape
    entries, parts = factor_blocks.shape[:2]
    span = factor_blocks.shape[-1]
    rows = parts * height
    columns = total_columns // parts
    cores = 2
    chips = span // (height * cores)
    packed = (parts - 1) * height
    factor = factor_blocks.reshape(entries, rows, span)
    inverse = diag_inverses.reshape(blocks, rows, span)
    block_rows, block_cols = block_index[:, 0], block_index[:, 1]
    numbers = jnp.arange(blocks, dtype=jnp.int32)
    match = (block_rows[None, None, :] == numbers[:, None, None]) & (
        block_cols[None, None, :] == numbers[None, :, None]
    )
    places = jnp.arange(1, entries + 1, dtype=jnp.int32)
    table = jnp.sum(jnp.where(match, places, 0), axis=2) - 1

    wholes = jax.ShapeDtypeStruct((parts - 1, span, LANES), jnp.bfloat16)
    copies_shape = pltpu.VMEM((chips, packed, LANES), jnp.bfloat16)
    pieces_shape = pltpu.VMEM((parts, blocks, height, columns), jnp.bfloat16)
    history_shape = pltpu.HBM((blocks - 2,) + wholes.shape, jnp.bfloat16)
    whole_scratch = pltpu.VMEM(wholes.shape, jnp.bfloat16)
    matrix_scratch = pltpu.VMEM((parts, rows, span), jnp.bfloat16)
    wide_scratch = pltpu.VMEM((rows, LANES), jnp.float32)

    def most(last):
        return min(entries, last * (last + 1) // 2)

    bounds = [0] + [most(last) for _, last in CHUNK_ROWS]
    bounds[-2] = (bounds[-3] + entries) // 2
    sizes = [last + 1 - first for first, last in CHUNK_ROWS]
    spans = [(low, high, size) for low, high, size in zip(bounds, bounds[1:], sizes)]
    chunks = [None] * len(spans)

    def gather_chunk(number, after):
        first, last = CHUNK_ROWS[number]
        low, high, _ = spans[number]
        slab = jnp.concatenate([inverse[first : last + 1], factor[low:high]], axis=0)
        if after is not None:
            slab, after = lax.optimization_barrier((slab, after))
        chunks[number] = lax.all_gather(slab, ROWS, axis=0)

    def chunks_of(current):
        high = most(current)
        low = max(0, entries - sum(range(current, blocks)))
        return [k for k, (a, b, _) in enumerate(spans) if a < high and b > low]

    def first(split):
        return pl.pallas_call(
            first_kernel,
            out_shape=copies_shape,
            in_specs=[vmem()],
            out_specs=vmem(),
            scratch_shapes=[wide_scratch],
            compiler_params=LIMIT,
            name="first",
        )(in_vmem(split))

    def solve(current, gathered, pieces):
        number = next(k for k, (a, b) in enumerate(CHUNK_ROWS) if a <= current <= b)
        place = current - CHUNK_ROWS[number][0]
        operands = [in_vmem(gathered), in_hbm(chunks[number])] + ([in_vmem(pieces)] if current else [])
        return pl.pallas_call(
            lambda *refs: solve_kernel(current, place, *refs),
            out_shape=(copies_shape, pieces_shape),
            in_specs=[vmem(), anywhere()] + ([vmem()] if current else []),
            out_specs=(vmem(), vmem()),
            input_output_aliases={2: 1} if current else {},
            scratch_shapes=[
                whole_scratch,
                matrix_scratch,
                pltpu.SemaphoreType.DMA,
            ],
            compiler_params=LIMIT,
            name="solve",
        )(*operands)

    def residual(current, gathered, split, earlier, history):
        used = chunks_of(current)
        keeps = current + 1 < blocks
        tail = [in_vmem(earlier)] if current > 1 else []
        if keeps and current > 1:
            tail.append(in_hbm(history))
        return pl.pallas_call(
            lambda *refs: residual_kernel(current, [spans[k] for k in used], *refs),
            out_shape=(copies_shape, history_shape) if keeps else (copies_shape,),
            in_specs=[smem(), vmem(), vmem()]
            + [anywhere()] * len(used)
            + [vmem(), anywhere()][: len(tail)],
            out_specs=(vmem(), anywhere()) if keeps else (vmem(),),
            input_output_aliases={4 + len(used): 1} if len(tail) > 1 else {},
            scratch_shapes=[
                whole_scratch,
                matrix_scratch,
                wide_scratch,
                wide_scratch,
                pltpu.SemaphoreType.DMA((2,)),
            ],
            compiler_params=LIMIT,
            name="residual",
        )(
            table[current],
            in_vmem(gathered),
            in_vmem(split),
            *[in_hbm(chunks[k]) for k in used],
            *tail,
        )

    def update(current, history):
        used = chunks_of(current)
        count = current - 1
        return pl.pallas_call(
            lambda *refs: update_kernel([spans[k] for k in used], *refs),
            out_shape=pltpu.VMEM((rows, LANES), jnp.float32),
            in_specs=[smem(), anywhere()] + [anywhere()] * len(used),
            out_specs=vmem(),
            scratch_shapes=[
                pltpu.VMEM((count,) + wholes.shape, jnp.bfloat16),
                pltpu.VMEM((count, parts, rows, span), jnp.bfloat16),
                pltpu.VMEM((parts - 1, 2 * rows, LANES), jnp.float32),
                pltpu.SemaphoreType.DMA((count,)),
                pltpu.SemaphoreType.DMA((count,)),
            ],
            compiler_params=LIMIT,
            cost_estimate=pl.CostEstimate(
                flops=count * 2 * rows * parts * span * 256,
                bytes_accessed=count * parts * span * (rows + LANES) * 2,
                transcendentals=0,
            ),
            name="update",
        )(table[current], in_hbm(history), *[in_hbm(chunks[k]) for k in used])

    split = rhs.reshape(blocks, height, parts, columns).transpose(2, 0, 1, 3)
    split = lax.all_to_all(split, ROWS, 0, 0, tiled=True)
    for number, after in enumerate(CHUNK_AFTER):
        if after is None:
            gather_chunk(number, None)
    copies = first(split)
    history = pieces = earlier = None
    for current in range(blocks):
        gathered = spread(copies)
        for number, after in enumerate(CHUNK_AFTER):
            if after == current:
                gather_chunk(number, gathered)
        copies, pieces = solve(current, gathered, pieces)
        if current + 1 == blocks:
            break
        if current:
            earlier = update(current + 1, history)
        gathered = spread(copies)
        copies, *history_after = residual(current + 1, gathered, split, earlier, history)
        history = history_after[0] if history_after else None

    out = lax.all_to_all(pieces, ROWS, 0, 0, tiled=True)
    return out.transpose(1, 2, 0, 3).reshape(blocks, height, total_columns)


def solution(mesh):
    cores = 2
    across, along = mesh.shape["prow"], mesh.shape["pcol"]
    grid = Mesh(mesh.devices.reshape(across, along // cores, cores), (ROWS, CHIPS, CORES))
    column = (CHIPS, CORES)
    in_specs = (
        P(None, (ROWS, CHIPS, CORES), None),
        P(None, None, column, None, ROWS),
        P(None, None, column, None, ROWS),
        P(),
    )
    out_specs = P(None, (ROWS, CHIPS, CORES), None)
    return jax.shard_map(shards, mesh=grid, in_specs=in_specs, out_specs=out_specs, check_vma=False)
```

time: 2180 us -> 621 us (0.28)
  blocking collectives: 1240 us -> 332 us
  loops' own time: 318 us -> 0 us
  waiting for transfers between devices: 420 us -> 116 us
  matrix products: 91.3 us -> 0 us
  Pallas kernels: 0 us -> 87.8 us
  local copies, waits for them, and re-layouts: 68.5 us -> 7.34 us
  starting transfers between devices: 0.58 us -> 52 us
    all_gather x23, blocking collectives: 1240 us -> 102 us  [spread(): return lax.all_gather(received, CORES, axis=0)]
    reduce_scatter x24 -> x0, waiting for transfers between devices: 419 us -> none  [the longest x12 213 us: finish_block(): lax.psum_scatter(partial_value, 'prow', scatter_dimension=0, tiled=True)]
    another operation x13 -> x0, loops' own time: 318 us -> none  [the longest x12 317 us: row_update(): lax.fori_loop(row_begin[current], row_end[current], accumulate, jnp.zeros...]
    all_to_all x0 -> x14, blocking collectives: none -> 230 us  [the longest x12 213 us: spread(): received = lax.all_to_all(copies, CHIPS, 0, 0, tiled=True)]
    all_to_all x0 -> x11, waiting for transfers between devices: none -> 115 us  [spread(): received = lax.all_to_all(copies, CHIPS, 0, 0, tiled=True)]
    dot_general x60 -> x0, matrix products: 91.3 us -> none  [the longest x48 70.7 us: accumulate(): return running + jnp.dot(matrix, source, preferred_element_type=jnp.float32)]
    pallas_call x0 -> x34, Pallas kernels: none -> 87.8 us  [the longest x10 36.6 us: update(): pl.pallas_call(lambda *refs: update_kernel([spans[k] for k in used], *ref...]
    all_to_all x0 -> x11, starting transfers between devices: none -> 51.8 us  [spread(): received = lax.all_to_all(copies, CHIPS, 0, 0, tiled=True)]
  transfers between devices with their start and end apart: 24 -> 17, of which waited for: 24 -> 11; matrix products, arithmetic and copies ran while one was open for 0% -> 1% of each run, Pallas kernels for 0% -> 11%
where the time goes in v2:
time: 621 us; the launch traced here: 617 us
  blocking collectives  332 us (53%)
  waiting for transfers between devices  116 us (19%)
  Pallas kernels  87.8 us (14%)
  starting transfers between devices  52 us (8%)
  between operations  14 us (2%)
  other arithmetic  7.39 us (1%)
  local copies, waits for them, and re-layouts  7.34 us (1%)
    all_to_all x12, blocking collectives, spread(): received = lax.all_to_all(copies, CHIPS, 0, 0, tiled=True)  213 us
    all_to_all x11, waiting for transfers between devices, spread(): received = lax.all_to_all(copies, CHIPS, 0, 0, tiled=True)  115 us
    all_gather x23, blocking collectives, spread(): return lax.all_gather(received, CORES, axis=0)  102 us
    all_to_all x11, starting transfers between devices, spread(): received = lax.all_to_all(copies, CHIPS, 0, 0, tiled=True)  51.8 us
    pallas_call x10, Pallas kernels, update(): pl.pallas_call(lambda *refs: update_kernel([spans[k] for k in used], *ref...  36.6 us
    pallas_call x11, Pallas kernels, residual(): pl.pallas_call(lambda *refs: residual_kernel(current, [spans[k] for k in...  25.4 us
    pallas_call x12, Pallas kernels, solve(): pl.pallas_call(lambda *refs: solve_kernel(current, place, *refs), out_sha...  24.9 us
  transfers between devices with their start and end apart: 17, of which 11 were waited for; matrix products, arithmetic and copies ran while one was open for 1% of the time, Pallas kernels for 11%

profile of v2, /device:TPU:1, one launch (start us, length us, event | category | flops | bytes accessed | tf_op | source)
XLA Modules:
  0.0 616.5 jit_solution(4440777963673257534)
XLA Ops:
  11.3 10.0 %all_to_all.125.rhs.refs_2_ = bf16[4,12,16,96]{3,2,1,0:T(8,128)(2,1)S(1)} all-to-all(bf16[4,12,16,96]{3,2,1,0:T(8,128)(2,1)S(1)} %bitcast.175), channel_id=1, replica_groups=mesh['prow'=4,'chip'=32,'core'=2] {'prow'}, dimensions={0} | all-to-all | bytes 294912 | tf_op jit(solution)/shard_map/all_to_all | solution.py:347
  22.2 11.2 %all-to-all-start.1 = ((bf16[32,48,128]{2,1,0:T(8,128)(2,1)}), bf16[32,48,128]{2,1,0:T(8,128)(2,1)S(1)}, u32[]{:S(2)}, u32[]{:S(2)}) async-start(bf16[32,48,128]{2,1,0:T(8,128)(2,1)} %first.1), calls=%async_computation.1 | async-start | bytes 786432 | tf_op jit(solution)/shard_map/all_to_all | solution.py:15
  34.6 10.4 %all-to-all-done.1 = bf16[32,48,128]{2,1,0:T(8,128)(2,1)S(1)} async-done(((bf16[32,48,128]{2,1,0:T(8,128)(2,1)}), bf16[32,48,128]{2,1,0:T(8,128)(2,1)S(1)}, u32[]{:S(2)}, u32[]{:S(2)}) %all-to-all-start.1) | async-done | bytes 393248 | tf_op jit(solution)/shard_map/all_to_all | solution.py:15
  58.4 13.5 %all-to-all-done.2 = bf16[32,48,128]{2,1,0:T(8,128)(2,1)S(1)} async-done(((bf16[32,48,128]{2,1,0:T(8,128)(2,1)}), bf16[32,48,128]{2,1,0:T(8,128)(2,1)S(1)}, u32[]{:S(2)}, u32[]{:S(2)}) %all-to-all-start.2) | async-done | bytes 393248 | tf_op jit(solution)/shard_map/all_to_all | solution.py:15
  78.5 17.7 %all_to_all.126 = bf16[32,48,128]{2,1,0:T(8,128)(2,1)S(1)} all-to-all(bf16[32,48,128]{2,1,0:T(8,128)(2,1)S(1)} %get-tuple-element.53), channel_id=1, replica_groups=mesh['prow'=4,'chip'=32,'core'=2] {'chip'}, dimensions={0} | all-to-all | bytes 786432 | tf_op jit(solution)/shard_map/all_to_all | solution.py:15
  102.1 17.7 %all_to_all.127 = bf16[32,48,128]{2,1,0:T(8,128)(2,1)S(1)} all-to-all(bf16[32,48,128]{2,1,0:T(8,128)(2,1)S(1)} %get-tuple-element.55), channel_id=1, replica_groups=mesh['prow'=4,'chip'=32,'core'=2] {'chip'}, dimensions={0} | all-to-all | bytes 786432 | tf_op jit(solution)/shard_map/all_to_all | solution.py:15
  134.2 10.9 %all-to-all-done.5 = bf16[32,48,128]{2,1,0:T(8,128)(2,1)S(1)} async-done(((bf16[32,48,128]{2,1,0:T(8,128)(2,1)}), bf16[32,48,128]{2,1,0:T(8,128)(2,1)S(1)}, u32[]{:S(2)}, u32[]{:S(2)}) %all-to-all-start.5) | async-done | bytes 393248 | tf_op jit(solution)/shard_map/all_to_all | solution.py:15
  158.5 11.2 %all-to-all-done.6 = bf16[32,48,128]{2,1,0:T(8,128)(2,1)S(1)} async-done(((bf16[32,48,128]{2,1,0:T(8,128)(2,1)}), bf16[32,48,128]{2,1,0:T(8,128)(2,1)S(1)}, u32[]{:S(2)}, u32[]{:S(2)}) %all-to-all-start.6) | async-done | bytes 393248 | tf_op jit(solution)/shard_map/all_to_all | solution.py:15
  176.3 17.7 %all_to_all.128 = bf16[32,48,128]{2,1,0:T(8,128)(2,1)S(1)} all-to-all(bf16[32,48,128]{2,1,0:T(8,128)(2,1)S(1)} %get-tuple-element.61), channel_id=1, replica_groups=mesh['prow'=4,'chip'=32,'core'=2] {'chip'}, dimensions={0} | all-to-all | bytes 786432 | tf_op jit(solution)/shard_map/all_to_all | solution.py:15
  199.9 17.7 %all_to_all.129 = bf16[32,48,128]{2,1,0:T(8,128)(2,1)S(1)} all-to-all(bf16[32,48,128]{2,1,0:T(8,128)(2,1)S(1)} %get-tuple-element.63), channel_id=1, replica_groups=mesh['prow'=4,'chip'=32,'core'=2] {'chip'}, dimensions={0} | all-to-all | bytes 786432 | tf_op jit(solution)/shard_map/all_to_all | solution.py:15
  235.2 10.5 %all-to-all-done.9 = bf16[32,48,128]{2,1,0:T(8,128)(2,1)S(1)} async-done(((bf16[32,48,128]{2,1,0:T(8,128)(2,1)}), bf16[32,48,128]{2,1,0:T(8,128)(2,1)S(1)}, u32[]{:S(2)}, u32[]{:S(2)}) %all-to-all-start.9) | async-done | bytes 393248 | tf_op jit(solution)/shard_map/all_to_all | solution.py:15
  260.5 9.9 %all-to-all-done.10 = bf16[32,48,128]{2,1,0:T(8,128)(2,1)S(1)} async-done(((bf16[32,48,128]{2,1,0:T(8,128)(2,1)}), bf16[32,48,128]{2,1,0:T(8,128)(2,1)S(1)}, u32[]{:S(2)}, u32[]{:S(2)}) %all-to-all-start.10) | async-done | bytes 393248 | tf_op jit(solution)/shard_map/all_to_all | solution.py:15
  277.0 17.7 %all_to_all.130 = bf16[32,48,128]{2,1,0:T(8,128)(2,1)S(1)} all-to-all(bf16[32,48,128]{2,1,0:T(8,128)(2,1)S(1)} %get-tuple-element.70), channel_id=1, replica_groups=mesh['prow'=4,'chip'=32,'core'=2] {'chip'}, dimensions={0} | all-to-all | bytes 786432 | tf_op jit(solution)/shard_map/all_to_all | solution.py:15
  300.7 17.7 %all_to_all.131 = bf16[32,48,128]{2,1,0:T(8,128)(2,1)S(1)} all-to-all(bf16[32,48,128]{2,1,0:T(8,128)(2,1)S(1)} %get-tuple-element.72), channel_id=1, replica_groups=mesh['prow'=4,'chip'=32,'core'=2] {'chip'}, dimensions={0} | all-to-all | bytes 786432 | tf_op jit(solution)/shard_map/all_to_all | solution.py:15
  334.8 12.5 %all-to-all-done.13 = bf16[32,48,128]{2,1,0:T(8,128)(2,1)S(1)} async-done(((bf16[32,48,128]{2,1,0:T(8,128)(2,1)}), bf16[32,48,128]{2,1,0:T(8,128)(2,1)S(1)}, u32[]{:S(2)}, u32[]{:S(2)}) %all-to-all-start.13) | async-done | bytes 393248 | tf_op jit(solution)/shard_map/all_to_all | solution.py:15
  362.7 9.3 %all-to-all-done.14 = bf16[32,48,128]{2,1,0:T(8,128)(2,1)S(1)} async-done(((bf16[32,48,128]{2,1,0:T(8,128)(2,1)}), bf16[32,48,128]{2,1,0:T(8,128)(2,1)S(1)}, u32[]{:S(2)}, u32[]{:S(2)}) %all-to-all-start.14) | async-done | bytes 393248 | tf_op jit(solution)/shard_map/all_to_all | solution.py:15
  377.9 17.7 %all_to_all.132 = bf16[32,48,128]{2,1,0:T(8,128)(2,1)S(1)} all-to-all(bf16[32,48,128]{2,1,0:T(8,128)(2,1)S(1)} %get-tuple-element.79), channel_id=1, replica_groups=mesh['prow'=4,'chip'=32,'core'=2] {'chip'}, dimensions={0} | all-to-all | bytes 786432 | tf_op jit(solution)/shard_map/all_to_all | solution.py:15
  410.8 9.4 %all-to-all-done.16 = bf16[32,48,128]{2,1,0:T(8,128)(2,1)S(1)} async-done(((bf16[32,48,128]{2,1,0:T(8,128)(2,1)}), bf16[32,48,128]{2,1,0:T(8,128)(2,1)S(1)}, u32[]{:S(2)}, u32[]{:S(2)}) %all-to-all-start.16) | async-done | bytes 393248 | tf_op jit(solution)/shard_map/all_to_all | solution.py:15
  426.8 17.7 %all_to_all.133 = bf16[32,48,128]{2,1,0:T(8,128)(2,1)S(1)} all-to-all(bf16[32,48,128]{2,1,0:T(8,128)(2,1)S(1)} %get-tuple-element.84), channel_id=1, replica_groups=mesh['prow'=4,'chip'=32,'core'=2] {'chip'}, dimensions={0} | all-to-all | bytes 786432 | tf_op jit(solution)/shard_map/all_to_all | solution.py:15
  450.4 17.7 %all_to_all.134 = bf16[32,48,128]{2,1,0:T(8,128)(2,1)S(1)} all-to-all(bf16[32,48,128]{2,1,0:T(8,128)(2,1)S(1)} %get-tuple-element.86), channel_id=1, replica_groups=mesh['prow'=4,'chip'=32,'core'=2] {'chip'}, dimensions={0} | all-to-all | bytes 786432 | tf_op jit(solution)/shard_map/all_to_all | solution.py:15
  478.6 17.7 %all_to_all.135 = bf16[32,48,128]{2,1,0:T(8,128)(2,1)S(1)} all-to-all(bf16[32,48,128]{2,1,0:T(8,128)(2,1)S(1)} %get-tuple-element.89), channel_id=1, replica_groups=mesh['prow'=4,'chip'=32,'core'=2] {'chip'}, dimensions={0} | all-to-all | bytes 786432 | tf_op jit(solution)/shard_map/all_to_all | solution.py:15
  512.1 9.1 %all-to-all-done.20 = bf16[32,48,128]{2,1,0:T(8,128)(2,1)S(1)} async-done(((bf16[32,48,128]{2,1,0:T(8,128)(2,1)}), bf16[32,48,128]{2,1,0:T(8,128)(2,1)S(1)}, u32[]{:S(2)}, u32[]{:S(2)}) %all-to-all-start.20) | async-done | bytes 393248 | tf_op jit(solution)/shard_map/all_to_all | solution.py:15
  527.7 17.7 %all_to_all.136 = bf16[32,48,128]{2,1,0:T(8,128)(2,1)S(1)} all-to-all(bf16[32,48,128]{2,1,0:T(8,128)(2,1)S(1)} %get-tuple-element.93), channel_id=1, replica_groups=mesh['prow'=4,'chip'=32,'core'=2] {'chip'}, dimensions={0} | all-to-all | bytes 786432 | tf_op jit(solution)/shard_map/all_to_all | solution.py:15
  576.5 17.7 %all_to_all.137 = bf16[32,48,128]{2,1,0:T(8,128)(2,1)S(1)} all-to-all(bf16[32,48,128]{2,1,0:T(8,128)(2,1)S(1)} %residual.21), channel_id=1, replica_groups=mesh['prow'=4,'chip'=32,'core'=2] {'chip'}, dimensions={0} | all-to-all | bytes 786432 | tf_op jit(solution)/shard_map/all_to_all | solution.py:15
  (123 shorter events, 262.2 us)
Async XLA Ops:
  6.5 2.3 slice-start
  6.5 45.2 %all-gather.36.cloned.1.call-start = ((), (), s32[]{:S(2)}) async-start(), calls=%async_computation.25 | async-start | bytes 1966080 | tf_op jit(solution)/shard_map/all_gather | solution.py:254
  9.7 114.5 %all-gather.38.cloned.1.call-start = ((), (), s32[]{:S(2)}) async-start(), calls=%async_computation.26 | async-start | bytes 4587520 | tf_op jit(solution)/shard_map/all_gather | solution.py:254
  22.2 11.2 %slice-start.2 = ((bf16[48,4,1,16,1024]{4,3,2,1,0:T(8,128)(2,1)}), bf16[9,4,1,16,1024]{4,3,2,1,0:T(8,128)(2,1)S(1)}, s32[]{:S(2)}) async-start(bf16[48,4,1,16,1024]{4,3,2,1,0:T(8,128)(2,1)} %param.5), calls=%async_computation.33 | async-start | bytes 2359296 | tf_op jit(solution)/shard_map/slice | solution.py:251
  22.2 22.8 %all-to-all-start.1 = ((bf16[32,48,128]{2,1,0:T(8,128)(2,1)}), bf16[32,48,128]{2,1,0:T(8,128)(2,1)S(1)}, u32[]{:S(2)}, u32[]{:S(2)}) async-start(bf16[32,48,128]{2,1,0:T(8,128)(2,1)} %first.1), calls=%async_computation.1 | async-start | bytes 786432 | tf_op jit(solution)/shard_map/all_to_all | solution.py:15
  33.4 188.6 %all-gather.40.cloned.1.call-start = ((), (), s32[]{:S(2)}) async-start(), calls=%async_computation.27 | async-start | bytes 7208960 | tf_op jit(solution)/shard_map/all_gather | solution.py:254
  34.6 17.0 %copy-start.4 = (s32[48,2]{0,1:T(2,128)S(1)}, s32[48,2]{0,1:T(2,128)}, u32[]{:S(2)}) copy-start(s32[48,2]{0,1:T(2,128)} %param.7) | copy-start | bytes 1156
  54.1 17.9 %all-to-all-start.2 = ((bf16[32,48,128]{2,1,0:T(8,128)(2,1)}), bf16[32,48,128]{2,1,0:T(8,128)(2,1)S(1)}, u32[]{:S(2)}, u32[]{:S(2)}) async-start(bf16[32,48,128]{2,1,0:T(8,128)(2,1)} %get-tuple-element.52), calls=%async_computation.2 | async-start | bytes 786432 | tf_op jit(solution)/shard_map/all_to_all | solution.py:15
  127.2 17.9 %all-to-all-start.5 = ((bf16[32,48,128]{2,1,0:T(8,128)(2,1)}), bf16[32,48,128]{2,1,0:T(8,128)(2,1)S(1)}, u32[]{:S(2)}, u32[]{:S(2)}) async-start(bf16[32,48,128]{2,1,0:T(8,128)(2,1)} %get-tuple-element.57), calls=%async_computation.5 | async-start | bytes 786432 | tf_op jit(solution)/shard_map/all_to_all | solution.py:15
  131.2 1.5 slice-start.3
  131.2 1.5 copy-start.2
  131.2 191.5 %all-gather.42.cloned.1.call-start = ((), (), s32[]{:S(2)}) async-start(), calls=%async_computation.28 | async-start | bytes 9830400 | tf_op jit(solution)/shard_map/all_gather | solution.py:254
  151.8 17.9 %all-to-all-start.6 = ((bf16[32,48,128]{2,1,0:T(8,128)(2,1)}), bf16[32,48,128]{2,1,0:T(8,128)(2,1)S(1)}, u32[]{:S(2)}, u32[]{:S(2)}) async-start(bf16[32,48,128]{2,1,0:T(8,128)(2,1)} %get-tuple-element.59), calls=%async_computation.6 | async-start | bytes 786432 | tf_op jit(solution)/shard_map/all_to_all | solution.py:15
  227.7 18.0 %all-to-all-start.9 = ((bf16[32,48,128]{2,1,0:T(8,128)(2,1)}), bf16[32,48,128]{2,1,0:T(8,128)(2,1)S(1)}, u32[]{:S(2)}, u32[]{:S(2)}) async-start(bf16[32,48,128]{2,1,0:T(8,128)(2,1)} %get-tuple-element.66), calls=%async_computation.9 | async-start | bytes 786432 | tf_op jit(solution)/shard_map/all_to_all | solution.py:15
  231.8 2.1 copy-start.1
  231.8 174.6 %all-gather.44.cloned.1.call-start = ((), (), s32[]{:S(2)}) async-start(), calls=%async_computation.29 | async-start | bytes 7864320 | tf_op jit(solution)/shard_map/all_gather | solution.py:254
  252.3 18.1 %all-to-all-start.10 = ((bf16[32,48,128]{2,1,0:T(8,128)(2,1)}), bf16[32,48,128]{2,1,0:T(8,128)(2,1)S(1)}, u32[]{:S(2)}, u32[]{:S(2)}) async-start(bf16[32,48,128]{2,1,0:T(8,128)(2,1)} %get-tuple-element.68), calls=%async_computation.10 | async-start | bytes 786432 | tf_op jit(solution)/shard_map/all_to_all | solution.py:15
  326.4 7.1 %copy-start = (bf16[2,4,1,16,1024]{4,3,2,1,0:T(8,128)(2,1)S(1)}, bf16[2,4,1,16,1024]{4,3,2,1,0:T(8,128)(2,1)}, u32[]{:S(2)}) copy-start(bf16[2,4,1,16,1024]{4,3,2,1,0:T(8,128)(2,1)} %get-tuple-element.101) | copy-start | bytes 786436
  329.4 17.9 %all-to-all-start.13 = ((bf16[32,48,128]{2,1,0:T(8,128)(2,1)}), bf16[32,48,128]{2,1,0:T(8,128)(2,1)S(1)}, u32[]{:S(2)}, u32[]{:S(2)}) async-start(bf16[32,48,128]{2,1,0:T(8,128)(2,1)} %get-tuple-element.75), calls=%async_computation.13 | async-start | bytes 786432 | tf_op jit(solution)/shard_map/all_to_all | solution.py:15
  333.5 139.0 %all-gather.46.cloned.1.call-start = ((), (), s32[]{:S(2)}) async-start(), calls=%async_computation.30 | async-start | bytes 7864320 | tf_op jit(solution)/shard_map/all_gather | solution.py:254
  354.1 17.9 %all-to-all-start.14 = ((bf16[32,48,128]{2,1,0:T(8,128)(2,1)}), bf16[32,48,128]{2,1,0:T(8,128)(2,1)S(1)}, u32[]{:S(2)}, u32[]{:S(2)}) async-start(bf16[32,48,128]{2,1,0:T(8,128)(2,1)} %get-tuple-element.77), calls=%async_computation.14 | async-start | bytes 786432 | tf_op jit(solution)/shard_map/all_to_all | solution.py:15
  402.3 17.9 %all-to-all-start.16 = ((bf16[32,48,128]{2,1,0:T(8,128)(2,1)}), bf16[32,48,128]{2,1,0:T(8,128)(2,1)S(1)}, u32[]{:S(2)}, u32[]{:S(2)}) async-start(bf16[32,48,128]{2,1,0:T(8,128)(2,1)} %get-tuple-element.81), calls=%async_computation.16 | async-start | bytes 786432 | tf_op jit(solution)/shard_map/all_to_all | solution.py:15
  503.2 17.9 %all-to-all-start.20 = ((bf16[32,48,128]{2,1,0:T(8,128)(2,1)}), bf16[32,48,128]{2,1,0:T(8,128)(2,1)S(1)}, u32[]{:S(2)}, u32[]{:S(2)}) async-start(bf16[32,48,128]{2,1,0:T(8,128)(2,1)} %get-tuple-element.91), calls=%async_computation.20 | async-start | bytes 786432 | tf_op jit(solution)/shard_map/all_to_all | solution.py:15
  552.1 17.9 %all-to-all-start.22 = ((bf16[32,48,128]{2,1,0:T(8,128)(2,1)}), bf16[32,48,128]{2,1,0:T(8,128)(2,1)S(1)}, u32[]{:S(2)}, u32[]{:S(2)}) async-start(bf16[32,48,128]{2,1,0:T(8,128)(2,1)} %get-tuple-element.95), calls=%async_computation.22 | async-start | bytes 786432 | tf_op jit(solution)/shard_map/all_to_all | solution.py:15
  (2 other events, 2.6 us)
Sparse Core Ops, SparseCore 0:
  9.8 32.8 all-gather.35
  44.6 46.5 all-gather.37
  93.0 64.1 all-gather.39
  158.8 81.9 all-gather.41
  250.1 62.0 all-gather.43
  351.8 62.0 all-gather.45
